TPU v7x, 32 devices: a whole 2x2x4 slice. The times are simulated.
32 devices in a mesh: tm: 8 (over y, x, core), inner: 4 (over z).
Axes of the slice: x: 2, y: 2, z: 4, core: 2. Of those that a mesh axis runs over, the one named last changes fastest.
Arguments:
- query_input: bfloat16 [4096, 1792], P(('tm', 'inner')), may hold values from -6 to 6
- key_input: bfloat16 [4096, 1792], P(('tm', 'inner')), may hold values from -6 to 6
- value_input: bfloat16 [4096, 1792], P(('tm', 'inner')), may hold values from -6 to 6
- cotangent: bfloat16 [4096, 1792], P(('tm', 'inner')), may hold values from -6 to 6
- span_labels: int32 [4096], P(('tm', 'inner')), may hold values from 0 to 6, as said below
Outputs:
- query_gradient: bfloat16 [4096, 1792], P(('tm', 'inner'))
- key_gradient: bfloat16 [4096, 1792], P(('tm', 'inner'))
- value_gradient: bfloat16 [4096, 1792], P(('tm', 'inner'))
Inputs may be any that keep to these rules, and one draw needn't show every extreme that they name: `span_labels`: span labels never fall along the tokens; each of the 7 spans holds 1 to 8 whole frames of 128 tokens and begins at a multiple of 128; one span holds exactly 1024 tokens.
All inputs are finite; a program needn't handle non-finite values.
Results may differ from a plain program's by a relative error of at most 0.008.
Values may be sent and summed in bfloat16 or wider, within the bound.
A program may use at most 192 MiB of HBM per device.

v0:
```python
import functools

import jax
import jax.numpy as jnp
from jax import lax
from jax.experimental import pallas as pl
from jax.experimental.pallas import tpu as pltpu
from jax.sharding import PartitionSpec as P

DH = 112
LANES = 128
HALF = 64
LOSS_SCALE = 1024.0
MASS = DH
LABEL = DH + 1


def mm(a, b, ca, cb):
    return lax.dot_general(
        a, b, (((ca,), (cb,)), ((), ())), preferred_element_type=jnp.float32
    )


def kernel(
    n, inner, heads,
    q_ref, k_ref, v_ref, c_ref, lab_ref,
    dq_ref, dk_ref, dv_ref,
    qp, kp, vp, cp,
    s1, r1, o1, w1, s2, r2, o2, w2, cum,
    send_sem, recv_sem, back_sem1, back_sem2,
):
    units = 2 * heads
    ratio = n // units
    me = lax.axis_index("tm") * inner + lax.axis_index("inner")
    unit = me // ratio
    tokens = q_ref.shape[0]
    lane_t = lax.broadcasted_iota(jnp.int32, (tokens, LANES), 1)
    lane_h = lax.broadcasted_iota(jnp.int32, (HALF, LANES), 1)
    lane_s = lax.broadcasted_iota(jnp.int32, (LANES, LANES), 1)

    def place(d):
        return {"tm": d // inner, "inner": d % inner}

    def send(src, dst, d, ssem, rsem):
        pltpu.make_async_remote_copy(
            src_ref=src, dst_ref=dst, send_sem=ssem, recv_sem=rsem,
            device_id=place(d), device_id_type=pl.DeviceIdType.MESH,
        ).start()

    def drain(ref, sem):
        pltpu.make_async_copy(ref, ref, sem).wait()

    barrier = pltpu.get_barrier_semaphore()

    def greet(i, carry):
        pl.semaphore_signal(
            barrier, inc=1, device_id=place((me + i) % n),
            device_id_type=pl.DeviceIdType.MESH,
        )
        return carry

    lax.fori_loop(1, n, greet, 0)

    def scatter(src, dst, ssem, rsem):
        if ratio == 1:
            pltpu.make_async_copy(src.at[me], dst.at[me], rsem).start()

            def one(i, carry):
                u = (me + i) % units
                send(src.at[u], dst.at[me], u, ssem, rsem)
                return carry

            lax.fori_loop(1, units, one, 0)
        else:

            def one(i, carry):
                u = (unit + i) % units

                @pl.when(u * ratio == me)
                def _():
                    pltpu.make_async_copy(src.at[u], dst.at[me], rsem).start()

                @pl.when(u * ratio != me)
                def _():
                    send(src.at[u], dst.at[me], u * ratio, ssem, rsem)

                return carry

            lax.fori_loop(0, units, one, 0)

    def scatter_end(src, ssem):
        if ratio == 1:
            drain(src.at[pl.ds(0, units - 1)], ssem)
        else:

            @pl.when(me % ratio == 0)
            def _():
                drain(src.at[pl.ds(0, units - 1)], ssem)

            @pl.when(me % ratio != 0)
            def _():
                drain(src.at[pl.ds(0, units)], ssem)

    def as_owner(fn):
        if ratio == 1:
            fn()
        else:
            pl.when(me % ratio == 0)(fn)

    def visible(got, out, back, ssem, rsem, bsem, reverse):
        def work():
            drain(got, rsem)

            def add(i, acc):
                d = n - 1 - i if reverse else i
                acc = acc + got[d].astype(jnp.float32)
                cum[d] = acc
                return acc

            last = lax.fori_loop(
                0, n, add, jnp.zeros((HALF, LANES), jnp.float32), unroll=4
            )

            def label(d):
                return jnp.broadcast_to(
                    got[d][:, LABEL : LABEL + 1].astype(jnp.float32), (HALF, LANES)
                )

            def pick(i, carry):
                cur, lab = carry
                d = i if reverse else n - 1 - i
                here = label(d)
                cur = jnp.where(here == lab, cur, cum[d])
                out[d] = jnp.where(lane_h == LABEL, 0.0, cur).astype(jnp.bfloat16)
                return cur, here

            first = label(0 if reverse else n - 1)
            lax.fori_loop(0, n, pick, (last, first), unroll=4)
            pltpu.make_async_copy(out.at[me], back.at[unit], bsem.at[unit]).start()

            def one(i, carry):
                d = (me + i) % n
                send(out.at[d], back.at[unit], d, ssem, bsem.at[unit])
                return carry

            lax.fori_loop(1, n, one, 0)

        as_owner(work)

    zero = jnp.zeros((tokens, LANES), jnp.bfloat16)
    ones = jnp.where(lane_t == MASS, 1.0, 0.0).astype(jnp.bfloat16)
    for h in range(heads):
        cols = slice(h * DH, (h + 1) * DH)
        qp[h] = zero
        kp[h] = zero
        cp[h] = zero
        vp[h] = ones
        kp[h, :, :DH] = jnp.maximum(k_ref[:, cols], 0)
        vp[h, :, :DH] = v_ref[:, cols]
    lab = jnp.broadcast_to(lab_ref[...].astype(jnp.float32), (LANES, LANES))

    def stage(dst, h, state):
        state = jnp.where(lane_s == LABEL, lab, state).astype(jnp.bfloat16)
        dst[2 * h] = state[:HALF]
        dst[2 * h + 1] = state[HALF:]

    for h in range(heads):
        stage(s1, h, mm(kp[h], vp[h], 0, 0))

    pl.semaphore_wait(barrier, n - 1)
    scatter(s1, r1, send_sem.at[0], recv_sem.at[0])
    for h in range(heads):
        cols = slice(h * DH, (h + 1) * DH)
        qp[h, :, :DH] = jnp.maximum(q_ref[:, cols], 0)
        cp[h, :, :DH] = c_ref[:, cols]
    visible(r1, o1, w1, send_sem.at[1], recv_sem.at[0], back_sem1, False)

    for h in range(heads):
        drain(w1.at[2 * h], back_sem1.at[2 * h])
        drain(w1.at[2 * h + 1], back_sem1.at[2 * h + 1])
        state = w1[2 * h : 2 * h + 2].reshape(LANES, LANES)
        query = qp[h]
        both = mm(query, state, 1, 0)
        inv = 1.0 / (both[:, MASS : MASS + 1] + float(DH))
        cot = cp[h].astype(jnp.float32) * LOSS_SCALE
        dot = jnp.sum(cot * both, axis=1, keepdims=True)
        back = jnp.where(lane_t == MASS, -(dot * inv) * inv, cot * inv)
        back = back.astype(jnp.bfloat16)
        stage(s2, h, mm(query, back, 0, 0))
        grad = mm(back, state, 1, 1)
        grad = jnp.where(query.astype(jnp.float32) > 0, grad, 0.0)
        dq_ref[:, h * DH : (h + 1) * DH] = grad.astype(jnp.bfloat16)[:, :DH]

    scatter(s2, r2, send_sem.at[2], recv_sem.at[1])
    visible(r2, o2, w2, send_sem.at[3], recv_sem.at[1], back_sem2, True)

    for h in range(heads):
        drain(w2.at[2 * h], back_sem2.at[2 * h])
        drain(w2.at[2 * h + 1], back_sem2.at[2 * h + 1])
        adjoint = w2[2 * h : 2 * h + 2].reshape(LANES, LANES)
        key = kp[h]
        grad = mm(vp[h], adjoint, 1, 1)
        grad = jnp.where(key.astype(jnp.float32) > 0, grad, 0.0)
        dk_ref[:, h * DH : (h + 1) * DH] = grad.astype(jnp.bfloat16)[:, :DH]
        grad = mm(key, adjoint, 1, 0)
        dv_ref[:, h * DH : (h + 1) * DH] = grad.astype(jnp.bfloat16)[:, :DH]

    scatter_end(s1, send_sem.at[0])
    scatter_end(s2, send_sem.at[2])

    def finish():
        drain(o1.at[pl.ds(0, n - 1)], send_sem.at[1])
        drain(o2.at[pl.ds(0, n - 1)], send_sem.at[3])

    as_owner(finish)


def local(query, key, value, cotangent, labels):
    tokens, width = query.shape
    heads = width // DH
    inner = lax.axis_size("inner")
    n = lax.axis_size("tm") * inner
    units = 2 * heads
    vmem = pl.BlockSpec(memory_space=pltpu.VMEM)
    shape = jax.ShapeDtypeStruct((tokens, width), jnp.bfloat16)
    padded = pltpu.VMEM((heads, tokens, LANES), jnp.bfloat16)
    per_unit = pltpu.VMEM((units, HALF, LANES), jnp.bfloat16)
    per_device = pltpu.VMEM((n, HALF, LANES), jnp.bfloat16)
    flops = 12 * heads * tokens * DH * DH
    return pl.pallas_call(
        functools.partial(kernel, n, inner, heads),
        out_shape=(shape, shape, shape),
        in_specs=[vmem] * 5,
        out_specs=(vmem, vmem, vmem),
        scratch_shapes=[
            padded, padded, padded, padded,
            per_unit, per_device, per_device, per_unit,
            per_unit, per_device, per_device, per_unit,
            pltpu.VMEM((n, HALF, LANES), jnp.float32),
            pltpu.SemaphoreType.DMA((4,)),
            pltpu.SemaphoreType.DMA((2,)),
            pltpu.SemaphoreType.DMA((units,)),
            pltpu.SemaphoreType.DMA((units,)),
        ],
        compiler_params=pltpu.CompilerParams(
            collective_id=0, has_side_effects=True, vmem_limit_bytes=48 * 2**20
        ),
        cost_estimate=pl.CostEstimate(
            flops=flops, bytes_accessed=14 * tokens * width, transcendentals=0
        ),
    )(query, key, value, cotangent, labels[:LANES].reshape(1, LANES))


def solution(mesh):
    rows = P(("tm", "inner"), None)
    return jax.shard_map(
        local,
        mesh=mesh,
        in_specs=(rows, rows, rows, rows, P(("tm", "inner"))),
        out_specs=(rows, rows, rows),
        check_vma=False,
    )
```

profile of v0, /device:TPU:0, one launch (start us, length us, event | category | flops | bytes accessed | tf_op | source)
XLA Modules:
  0.0 77.7 jit_solution(8337414240221134360)
XLA Ops:
  0.6 0.0 copy-start.4
  0.6 0.6 copy-done.4
  1.3 0.0 copy-start
  1.3 1.0 %copy-done = bf16[128,1792]{1,0:T(8,128)(2,1)S(1)} copy-done((bf16[128,1792]{1,0:T(8,128)(2,1)S(1)}, bf16[128,1792]{1,0:T(8,128)(2,1)}, u32[]{:S(2)}) %copy-start) | copy-done | bytes 458776
  2.3 0.0 copy-start.1
  2.3 1.0 %copy-done.1 = bf16[128,1792]{1,0:T(8,128)(2,1)S(1)} copy-done((bf16[128,1792]{1,0:T(8,128)(2,1)S(1)}, bf16[128,1792]{1,0:T(8,128)(2,1)}, u32[]{:S(2)}) %copy-start.1) | copy-done | bytes 458776
  3.3 0.0 copy-start.2
  3.3 1.0 %copy-done.2 = bf16[128,1792]{1,0:T(8,128)(2,1)S(1)} copy-done((bf16[128,1792]{1,0:T(8,128)(2,1)S(1)}, bf16[128,1792]{1,0:T(8,128)(2,1)}, u32[]{:S(2)}) %copy-start.2) | copy-done | bytes 458776
  4.3 0.0 copy-start.3
  4.3 1.0 %copy-done.3 = bf16[128,1792]{1,0:T(8,128)(2,1)S(1)} copy-done((bf16[128,1792]{1,0:T(8,128)(2,1)S(1)}, bf16[128,1792]{1,0:T(8,128)(2,1)}, u32[]{:S(2)}) %copy-start.3) | copy-done | bytes 458776
  5.4 70.0 %shard_map.76 = (bf16[128,1792]{1,0:T(8,128)(2,1)S(1)}, bf16[128,1792]{1,0:T(8,128)(2,1)S(1)}, bf16[128,1792]{1,0:T(8,128)(2,1)S(1)}) custom-call(bf16[128,1792]{1,0:T(8,128)(2,1)S(1)} %copy-done, bf16[128,1792]{1,0:T(8,128)(2,1)S(1)} %copy-done.1, bf16[128,1792]{1,0:T(8,128)(2,1)S(1)} %copy-done.2, bf16[128,1792]{1,0:T(8,128)(2,1)S(1)} %copy-done.3, ...), custom_call_target="tpu_custom_call" | custom-call | flops 308281344 | bytes 3211264 | tf_op jit(solution)/shard_map/pallas_call | solution.py:230
  75.4 0.8 copy.11
  76.2 0.8 copy.12
  77.0 0.8 copy.13
Async XLA Ops:
  0.6 0.7 copy-start.4
  1.3 1.0 %copy-start = (bf16[128,1792]{1,0:T(8,128)(2,1)S(1)}, bf16[128,1792]{1,0:T(8,128)(2,1)}, u32[]{:S(2)}) copy-start(bf16[128,1792]{1,0:T(8,128)(2,1)} %q_ref.1) | copy-start | bytes 1376260
  2.3 1.0 %copy-start.1 = (bf16[128,1792]{1,0:T(8,128)(2,1)S(1)}, bf16[128,1792]{1,0:T(8,128)(2,1)}, u32[]{:S(2)}) copy-start(bf16[128,1792]{1,0:T(8,128)(2,1)} %k_ref.1) | copy-start | bytes 1376260
  3.3 1.0 %copy-start.2 = (bf16[128,1792]{1,0:T(8,128)(2,1)S(1)}, bf16[128,1792]{1,0:T(8,128)(2,1)}, u32[]{:S(2)}) copy-start(bf16[128,1792]{1,0:T(8,128)(2,1)} %v_ref.1) | copy-start | bytes 1376260
  4.3 1.0 %copy-start.3 = (bf16[128,1792]{1,0:T(8,128)(2,1)S(1)}, bf16[128,1792]{1,0:T(8,128)(2,1)}, u32[]{:S(2)}) copy-start(bf16[128,1792]{1,0:T(8,128)(2,1)} %c_ref.1) | copy-start | bytes 1376260
where the time goes:
time: 78 us; the launch traced here: 77.7 us
  Pallas kernels  70 us (90%)
  local copies, waits for them, and re-layouts  7.02 us (9%)
    pallas_call x1, Pallas kernels, local(): pl.pallas_call(functools.partial(kernel, n, inner, heads), out_shape=(sha...  70 us
    unnamed x13, local copies, waits for them, and re-layouts  7.02 us

commit v1 on v0

v1 whole, which is shorter than its diff:
```python
import functools

import jax
import jax.numpy as jnp
from jax import lax
from jax.experimental import pallas as pl
from jax.experimental.pallas import tpu as pltpu
from jax.sharding import PartitionSpec as P

DH = 112
LANES = 128
HALF = 64
LOSS_SCALE = 1024.0
MASS = DH
LABEL = DH + 1


def mm(a, b, ca, cb):
    return lax.dot_general(
        a, b, (((ca,), (cb,)), ((), ())), preferred_element_type=jnp.float32
    )


GROUPS = 4
ROWS = (HALF, DH - HALF)


def kernel(
    n, inner, heads,
    q_hbm, k_hbm, v_hbm, c_hbm, lab_hbm,
    dq_ref, dk_ref, dv_ref,
    q_ref, k_ref, v_ref, c_ref, lab_ref,
    qp, kp, vp, cp, nb,
    s1, r1, o1, w1, s2, r2, o2, w2, cum,
    in_sem, send_sem, out_sem, recv_sem, back_sem1, back_sem2,
):
    units = 2 * heads
    ratio = n // units
    me = lax.axis_index("tm") * inner + lax.axis_index("inner")
    unit = me // ratio
    per_group = units // GROUPS
    group = unit // per_group
    tokens = q_hbm.shape[0]
    lane_t = lax.broadcasted_iota(jnp.int32, (tokens, LANES), 1)
    lane_s = lax.broadcasted_iota(jnp.int32, (LANES, LANES), 1)

    def place(d):
        return {"tm": d // inner, "inner": d % inner}

    def send(src, dst, d, ssem, rsem):
        pltpu.make_async_remote_copy(
            src_ref=src, dst_ref=dst, send_sem=ssem, recv_sem=rsem,
            device_id=place(d), device_id_type=pl.DeviceIdType.MESH,
        ).start()

    def drain(ref, sem):
        pltpu.make_async_copy(ref, ref, sem).wait()

    fetch = [
        pltpu.make_async_copy(a, b, in_sem.at[i])
        for i, (a, b) in enumerate(
            (
                (lab_hbm, lab_ref), (k_hbm, k_ref), (v_hbm, v_ref),
                (q_hbm, q_ref), (c_hbm, c_ref),
            )
        )
    ]
    for copy in fetch:
        copy.start()

    barrier = pltpu.get_barrier_semaphore()

    def greet(i, carry):
        pl.semaphore_signal(
            barrier, inc=1, device_id=place((me + i) % n),
            device_id_type=pl.DeviceIdType.MESH,
        )
        return carry

    lax.fori_loop(1, n, greet, 0)

    def each_group(fn):
        def step(i, carry):
            now = (group + GROUPS - i) % GROUPS
            for g in range(GROUPS):
                pl.when(now == g)(functools.partial(fn, g))
            return carry

        lax.fori_loop(0, GROUPS, step, 0)

    def post(src, dst, g, ssem, rsem):
        pairs = per_group // 2

        def one(j, carry):
            pair = (unit // 2 + j) % pairs
            for b, rows in enumerate(ROWS):
                u = per_group * g + 2 * pair + b
                here = src.at[u, pl.ds(0, rows)]
                there = dst.at[me, pl.ds(0, rows)]

                @pl.when(u * ratio == me)
                def _():
                    pltpu.make_async_copy(here, there, rsem).start()

                @pl.when(u * ratio != me)
                def _():
                    send(here, there, u * ratio, ssem.at[b], rsem)

            return carry

        lax.fori_loop(0, pairs, one, 0)

    def as_owner(fn):
        for b, rows in enumerate(ROWS):
            mine = unit % 2 == b
            if ratio > 1:
                mine = mine & (me % ratio == 0)
            pl.when(mine)(functools.partial(fn, b, rows))

    def post_end(src, ssem):
        def owner(b, rows):
            for a, size in enumerate(ROWS):
                count = heads - 1 if a == b else heads
                drain(src.at[pl.ds(0, count), pl.ds(0, size)], ssem.at[a])

        as_owner(owner)
        if ratio > 1:

            @pl.when(me % ratio != 0)
            def _():
                for a, size in enumerate(ROWS):
                    drain(src.at[pl.ds(0, heads), pl.ds(0, size)], ssem.at[a])

    def visible(got, out, back, ssem, rsem, bsem, reverse):
        def work(b, rows):
            drain(got.at[pl.ds(0, n), pl.ds(0, rows)], rsem)
            lane_r = lax.broadcasted_iota(jnp.int32, (rows, LANES), 1)

            def add(i, acc):
                d = n - 1 - i if reverse else i
                acc = acc + got[d, :rows].astype(jnp.float32)
                cum[d, :rows] = acc
                return acc

            last = lax.fori_loop(
                0, n, add, jnp.zeros((rows, LANES), jnp.float32), unroll=4
            )

            def label(d):
                column = got[d, :16, LABEL : LABEL + 1].astype(jnp.float32)
                wide = jnp.broadcast_to(column, (16, LANES))
                return jnp.concatenate([wide] * (rows // 16), axis=0)

            def pick(i, carry):
                cur, lab = carry
                d = i if reverse else n - 1 - i
                here = label(d)
                cur = jnp.where(here == lab, cur, cum[d, :rows])
                out[d, :rows] = jnp.where(lane_r == LABEL, 0.0, cur).astype(
                    jnp.bfloat16
                )
                return cur, here

            first = label(0 if reverse else n - 1)
            lax.fori_loop(0, n, pick, (last, first), unroll=4)
            part = pl.ds(0, rows)
            there = back.at[unit, part]
            pltpu.make_async_copy(out.at[me, part], there, bsem.at[unit]).start()
            block = n // GROUPS

            def one(i, carry):
                d = block * ((me // block + i // block) % GROUPS) + (me + i) % block
                send(out.at[d, part], there, d, ssem, bsem.at[unit])
                return carry

            lax.fori_loop(1, n, one, 0)

        as_owner(work)

    def arrive(back, bsem, h):
        for b, rows in enumerate(ROWS):
            u = 2 * h + b
            drain(back.at[u, pl.ds(0, rows)], bsem.at[u])

    zero = jnp.zeros((tokens, LANES), jnp.bfloat16)
    ones = jnp.where(lane_t == MASS, 1.0, 0.0).astype(jnp.bfloat16)
    blank = jnp.zeros((HALF - ROWS[1], LANES), jnp.bfloat16)
    for h in range(heads):
        qp[h] = zero
        kp[h] = zero
        cp[h] = zero
        vp[h] = ones
        w1[2 * h + 1, ROWS[1] :] = blank
        w2[2 * h + 1, ROWS[1] :] = blank
    for copy in fetch[:3]:
        copy.wait()
    lab = jnp.broadcast_to(lab_ref[...].astype(jnp.float32), (LANES, LANES))

    def stage(dst, h, state):
        state = jnp.where(lane_s == LABEL, lab, state).astype(jnp.bfloat16)
        dst[2 * h] = state[:HALF]
        dst[2 * h + 1] = state[HALF:]

    def members(g):
        return range(g * heads // GROUPS, (g + 1) * heads // GROUPS)

    for h in range(heads):
        cols = slice(h * DH, (h + 1) * DH)
        kp[h, :, :DH] = jnp.maximum(k_ref[:, cols], 0)
        vp[h, :, :DH] = v_ref[:, cols]
    pl.semaphore_wait(barrier, n - 1)

    def keys(g):
        for h in members(g):
            stage(s1, h, mm(kp[h], vp[h], 0, 0))
        post(s1, r1, g, send_sem.at[0], recv_sem.at[0])

    each_group(keys)

    for copy in fetch[3:]:
        copy.wait()
    for h in range(heads):
        cols = slice(h * DH, (h + 1) * DH)
        qp[h, :, :DH] = jnp.maximum(q_ref[:, cols], 0)
        cp[h, :, :DH] = c_ref[:, cols]
    visible(r1, o1, w1, out_sem.at[0], recv_sem.at[0], back_sem1, False)

    def queries(g):
        for h in members(g):
            arrive(w1, back_sem1, h)
        for h in members(g):
            state = w1[2 * h : 2 * h + 2].reshape(LANES, LANES)
            query = qp[h]
            both = mm(query, state, 1, 0)
            inv = 1.0 / (both[:, MASS : MASS + 1] + float(DH))
            cot = cp[h].astype(jnp.float32) * LOSS_SCALE
            dot = jnp.sum(cot * both, axis=1, keepdims=True)
            back = jnp.where(lane_t == MASS, -(dot * inv) * inv, cot * inv)
            back = back.astype(jnp.bfloat16)
            nb[h] = back
            stage(s2, h, mm(query, back, 0, 0))
        post(s2, r2, g, send_sem.at[1], recv_sem.at[1])

    each_group(queries)

    for h in range(heads):
        state = w1[2 * h : 2 * h + 2].reshape(LANES, LANES)
        grad = mm(nb[h], state, 1, 1)
        grad = jnp.where(qp[h].astype(jnp.float32) > 0, grad, 0.0)
        dq_ref[:, h * DH : (h + 1) * DH] = grad.astype(jnp.bfloat16)[:, :DH]
    visible(r2, o2, w2, out_sem.at[1], recv_sem.at[1], back_sem2, True)

    def values(g):
        for h in members(g):
            arrive(w2, back_sem2, h)
        for h in members(g):
            adjoint = w2[2 * h : 2 * h + 2].reshape(LANES, LANES)
            key = kp[h]
            grad = mm(vp[h], adjoint, 1, 1)
            grad = jnp.where(key.astype(jnp.float32) > 0, grad, 0.0)
            dk_ref[:, h * DH : (h + 1) * DH] = grad.astype(jnp.bfloat16)[:, :DH]
            grad = mm(key, adjoint, 1, 0)
            dv_ref[:, h * DH : (h + 1) * DH] = grad.astype(jnp.bfloat16)[:, :DH]

    each_group(values)

    post_end(s1, send_sem.at[0])
    post_end(s2, send_sem.at[1])

    def finish(b, rows):
        drain(o1.at[pl.ds(0, n - 1), pl.ds(0, rows)], out_sem.at[0])
        drain(o2.at[pl.ds(0, n - 1), pl.ds(0, rows)], out_sem.at[1])

    as_owner(finish)


def local(query, key, value, cotangent, labels):
    tokens, width = query.shape
    heads = width // DH
    inner = lax.axis_size("inner")
    n = lax.axis_size("tm") * inner
    units = 2 * heads
    vmem = pl.BlockSpec(memory_space=pltpu.VMEM)
    shape = jax.ShapeDtypeStruct((tokens, width), jnp.bfloat16)
    padded = pltpu.VMEM((heads, tokens, LANES), jnp.bfloat16)
    flat = pltpu.VMEM((tokens, width), jnp.bfloat16)
    per_unit = pltpu.VMEM((units, HALF, LANES), jnp.bfloat16)
    per_device = pltpu.VMEM((n, HALF, LANES), jnp.bfloat16)
    flops = 12 * heads * tokens * DH * DH
    return pl.pallas_call(
        functools.partial(kernel, n, inner, heads),
        out_shape=(shape, shape, shape),
        in_specs=[pl.BlockSpec(memory_space=pltpu.HBM)] * 5,
        out_specs=(vmem, vmem, vmem),
        scratch_shapes=[
            flat, flat, flat, flat, pltpu.VMEM((1, LANES), jnp.int32),
            padded, padded, padded, padded, padded,
            per_unit, per_device, per_device, per_unit,
            per_unit, per_device, per_device, per_unit,
            pltpu.VMEM((n, HALF, LANES), jnp.float32),
            pltpu.SemaphoreType.DMA((5,)),
            pltpu.SemaphoreType.DMA((2, 2)),
            pltpu.SemaphoreType.DMA((2,)),
            pltpu.SemaphoreType.DMA((2,)),
            pltpu.SemaphoreType.DMA((units,)),
            pltpu.SemaphoreType.DMA((units,)),
        ],
        compiler_params=pltpu.CompilerParams(
            collective_id=0, has_side_effects=True, vmem_limit_bytes=63 * 2**20
        ),
        cost_estimate=pl.CostEstimate(
            flops=flops, bytes_accessed=14 * tokens * width, transcendentals=0
        ),
    )(query, key, value, cotangent, labels[:LANES].reshape(1, LANES))


def solution(mesh):
    rows = P(("tm", "inner"), None)
    return jax.shard_map(
        local,
        mesh=mesh,
        in_specs=(rows, rows, rows, rows, P(("tm", "inner"))),
        out_specs=(rows, rows, rows),
        check_vma=False,
    )
```

time: 78 us -> 61 us (0.78)
  Pallas kernels: 70 us -> 56.3 us
  local copies, waits for them, and re-layouts: 7.02 us -> 3.82 us
    pallas_call x1, Pallas kernels: 70 us -> 56.3 us  [local(): pl.pallas_call(functools.partial(kernel, n, inner, heads), out_shape=(sha...]
    unnamed x13 -> x7, local copies, waits for them, and re-layouts: 7.02 us -> 3.82 us
where the time goes in v1:
time: 61 us; the launch traced here: 60.8 us
  Pallas kernels  56.3 us (92%)
  local copies, waits for them, and re-layouts  3.82 us (6%)
  between operations  0.65 us (1%)
    pallas_call x1, Pallas kernels, local(): pl.pallas_call(functools.partial(kernel, n, inner, heads), out_shape=(sha...  56.3 us
    unnamed x7, local copies, waits for them, and re-layouts  3.82 us

profile of v1, /device:TPU:0, one launch (start us, length us, event | category | flops | bytes accessed | tf_op | source)
XLA Modules:
  0.0 60.8 jit_solution(577186123819038811)
XLA Ops:
  0.6 56.3 %shard_map.76 = (bf16[128,1792]{1,0:T(8,128)(2,1)}, bf16[128,1792]{1,0:T(8,128)(2,1)}, bf16[128,1792]{1,0:T(8,128)(2,1)}) custom-call(bf16[128,1792]{1,0:T(8,128)(2,1)} %q_hbm.1, bf16[128,1792]{1,0:T(8,128)(2,1)} %k_hbm.1, bf16[128,1792]{1,0:T(8,128)(2,1)} %v_hbm.1, bf16[128,1792]{1,0:T(8,128)(2,1)} %c_hbm.1, s32[1,128]{1,0:T(1,128)} %bitcast.1), custom_call_target="tpu_custom_call" | custom-call | flops 308281344 | bytes 3211264 | tf_op jit(solution)/shard_map/pallas_call | solution.py:290
  56.9 0.0 copy-start.1
  56.9 1.9 %copy.11 = bf16[128,1792]{1,0:T(8,128)(2,1)} copy(bf16[128,1792]{1,0:T(8,128)(2,1)} %get-tuple-element.6) | data formatting | bytes 917504
  58.8 0.0 copy-done.1
  58.8 0.0 copy-start
  58.8 0.8 %copy.12 = bf16[128,1792]{1,0:T(8,128)(2,1)} copy(bf16[128,1792]{1,0:T(8,128)(2,1)S(1)} %copy-done.1) | data formatting | bytes 917504
  59.6 0.4 copy-done
  60.0 0.8 %copy.13 = bf16[128,1792]{1,0:T(8,128)(2,1)} copy(bf16[128,1792]{1,0:T(8,128)(2,1)S(1)} %copy-done) | data formatting | bytes 917504
Async XLA Ops:
  56.9 1.9 %copy-start.1 = (bf16[128,1792]{1,0:T(8,128)(2,1)S(1)}, bf16[128,1792]{1,0:T(8,128)(2,1)}, u32[]{:S(2)}) copy-start(bf16[128,1792]{1,0:T(8,128)(2,1)} %get-tuple-element.7) | copy-start | bytes 1376260
  58.8 1.2 %copy-start = (bf16[128,1792]{1,0:T(8,128)(2,1)S(1)}, bf16[128,1792]{1,0:T(8,128)(2,1)}, u32[]{:S(2)}) copy-start(bf16[128,1792]{1,0:T(8,128)(2,1)} %get-tuple-element.8) | copy-start | bytes 1376260

commit v2 on v1

--- a/solution.py
+++ b/solution.py
@@ -143,7 +143,7 @@
                 return acc
 
             last = lax.fori_loop(
-                0, n, add, jnp.zeros((rows, LANES), jnp.float32), unroll=4
+                0, n, add, jnp.zeros((rows, LANES), jnp.float32), unroll=8
             )
 
             def label(d):
@@ -162,7 +162,7 @@
                 return cur, here
 
             first = label(0 if reverse else n - 1)
-            lax.fori_loop(0, n, pick, (last, first), unroll=4)
+            lax.fori_loop(0, n, pick, (last, first), unroll=8)
             part = pl.ds(0, rows)
             there = back.at[unit, part]
             pltpu.make_async_copy(out.at[me, part], there, bsem.at[unit]).start()
@@ -204,13 +204,13 @@
     def members(g):
         return range(g * heads // GROUPS, (g + 1) * heads // GROUPS)
 
-    for h in range(heads):
-        cols = slice(h * DH, (h + 1) * DH)
-        kp[h, :, :DH] = jnp.maximum(k_ref[:, cols], 0)
-        vp[h, :, :DH] = v_ref[:, cols]
     pl.semaphore_wait(barrier, n - 1)
 
     def keys(g):
+        for h in members(g):
+            cols = slice(h * DH, (h + 1) * DH)
+            kp[h, :, :DH] = jnp.maximum(k_ref[:, cols], 0)
+            vp[h, :, :DH] = v_ref[:, cols]
         for h in members(g):
             stage(s1, h, mm(kp[h], vp[h], 0, 0))
         post(s1, r1, g, send_sem.at[0], recv_sem.at[0])

time: 61 us -> 60.5 us (level)
  no operation moved by 1% of the time
where the time goes in v2:
time: 60.5 us; the launch traced here: 60.3 us
  Pallas kernels  55.8 us (92%)
  local copies, waits for them, and re-layouts  3.82 us (6%)
  between operations  0.65 us (1%)
    pallas_call x1, Pallas kernels, local(): pl.pallas_call(functools.partial(kernel, n, inner, heads), out_shape=(sha...  55.8 us
    unnamed x7, local copies, waits for them, and re-layouts  3.82 us

profile of v2, /device:TPU:0, one launch (start us, length us, event | category | flops | bytes accessed | tf_op | source)
XLA Modules:
  0.0 60.3 jit_solution(5156638938765012480)
XLA Ops:
  0.6 55.8 %shard_map.76 = (bf16[128,1792]{1,0:T(8,128)(2,1)}, bf16[128,1792]{1,0:T(8,128)(2,1)}, bf16[128,1792]{1,0:T(8,128)(2,1)}) custom-call(bf16[128,1792]{1,0:T(8,128)(2,1)} %q_hbm.1, bf16[128,1792]{1,0:T(8,128)(2,1)} %k_hbm.1, bf16[128,1792]{1,0:T(8,128)(2,1)} %v_hbm.1, bf16[128,1792]{1,0:T(8,128)(2,1)} %c_hbm.1, s32[1,128]{1,0:T(1,128)} %bitcast.1), custom_call_target="tpu_custom_call" | custom-call | flops 308281344 | bytes 3211264 | tf_op jit(solution)/shard_map/pallas_call | solution.py:290
  56.5 0.0 copy-start.1
  56.5 1.9 %copy.11 = bf16[128,1792]{1,0:T(8,128)(2,1)} copy(bf16[128,1792]{1,0:T(8,128)(2,1)} %get-tuple-element.6) | data formatting | bytes 917504
  58.3 0.0 copy-done.1
  58.3 0.0 copy-start
  58.3 0.8 %copy.12 = bf16[128,1792]{1,0:T(8,128)(2,1)} copy(bf16[128,1792]{1,0:T(8,128)(2,1)S(1)} %copy-done.1) | data formatting | bytes 917504
  59.1 0.4 copy-done
  59.5 0.8 %copy.13 = bf16[128,1792]{1,0:T(8,128)(2,1)} copy(bf16[128,1792]{1,0:T(8,128)(2,1)S(1)} %copy-done) | data formatting | bytes 917504
Async XLA Ops:
  56.5 1.9 %copy-start.1 = (bf16[128,1792]{1,0:T(8,128)(2,1)S(1)}, bf16[128,1792]{1,0:T(8,128)(2,1)}, u32[]{:S(2)}) copy-start(bf16[128,1792]{1,0:T(8,128)(2,1)} %get-tuple-element.7) | copy-start | bytes 1376260
  58.3 1.2 %copy-start = (bf16[128,1792]{1,0:T(8,128)(2,1)S(1)}, bf16[128,1792]{1,0:T(8,128)(2,1)}, u32[]{:S(2)}) copy-start(bf16[128,1792]{1,0:T(8,128)(2,1)} %get-tuple-element.8) | copy-start | bytes 1376260

commit v3 on v2

--- a/solution.py
+++ b/solution.py
@@ -274,6 +274,32 @@
     as_owner(finish)
 
 
+PIECES = 2
+
+
+def deliver(*refs):
+    sources, results, held, get_sem, put_sem = refs[:3], refs[3:6], *refs[6:]
+    rows = sources[0].shape[0] // PIECES
+    gets, puts = [], []
+    for i in range(3):
+        for p in range(PIECES):
+            part = pl.ds(p * rows, rows)
+            slot = held.at[i, part]
+            gets.append(
+                pltpu.make_async_copy(sources[i].at[part], slot, get_sem.at[i, p])
+            )
+            puts.append(
+                pltpu.make_async_copy(slot, results[i].at[part], put_sem.at[i, p])
+            )
+    for copy in gets:
+        copy.start()
+    for get, put in zip(gets, puts):
+        get.wait()
+        put.start()
+    for copy in puts:
+        copy.wait()
+
+
 def local(query, key, value, cotangent, labels):
     tokens, width = query.shape
     heads = width // DH
@@ -287,7 +313,7 @@
     per_unit = pltpu.VMEM((units, HALF, LANES), jnp.bfloat16)
     per_device = pltpu.VMEM((n, HALF, LANES), jnp.bfloat16)
     flops = 12 * heads * tokens * DH * DH
-    return pl.pallas_call(
+    grads = pl.pallas_call(
         functools.partial(kernel, n, inner, heads),
         out_shape=(shape, shape, shape),
         in_specs=[pl.BlockSpec(memory_space=pltpu.HBM)] * 5,
@@ -312,6 +338,18 @@
             flops=flops, bytes_accessed=14 * tokens * width, transcendentals=0
         ),
     )(query, key, value, cotangent, labels[:LANES].reshape(1, LANES))
+    hbm = pl.BlockSpec(memory_space=pltpu.HBM)
+    return pl.pallas_call(
+        deliver,
+        out_shape=(shape, shape, shape),
+        in_specs=[hbm] * 3,
+        out_specs=(hbm, hbm, hbm),
+        scratch_shapes=[
+            pltpu.VMEM((3, tokens, width), jnp.bfloat16),
+            pltpu.SemaphoreType.DMA((3, PIECES)),
+            pltpu.SemaphoreType.DMA((3, PIECES)),
+        ],
+    )(*grads)
 
 
 def solution(mesh):

time: 60.5 us -> 58.9 us (0.974)
  local copies, waits for them, and re-layouts: 3.82 us -> 0 us
  Pallas kernels: 55.8 us -> 58.1 us
    unnamed x7 -> x0, local copies, waits for them, and re-layouts: 3.82 us -> none
    pallas_call x0 -> x1, Pallas kernels: none -> 2.22 us  [local(): pl.pallas_call(deliver, out_shape=(shape, shape, shape), in_specs=[hbm] *...]
where the time goes in v3:
time: 58.9 us; the launch traced here: 58.7 us
  Pallas kernels  58.1 us (99%)
  between operations  0.64 us (1%)
    pallas_call x1, Pallas kernels, local(): pl.pallas_call(functools.partial(kernel, n, inner, heads), out_shape=(sha...  55.8 us
    pallas_call x1, Pallas kernels, local(): pl.pallas_call(deliver, out_shape=(shape, shape, shape), in_specs=[hbm] *...  2.22 us

profile of v3, /device:TPU:0, one launch (start us, length us, event | category | flops | bytes accessed | tf_op | source)
XLA Modules:
  0.0 58.7 jit_solution(10658565095642120135)
XLA Ops:
  0.6 55.8 %shard_map.76 = (bf16[128,1792]{1,0:T(8,128)(2,1)}, bf16[128,1792]{1,0:T(8,128)(2,1)}, bf16[128,1792]{1,0:T(8,128)(2,1)}) custom-call(bf16[128,1792]{1,0:T(8,128)(2,1)} %q_hbm.1, bf16[128,1792]{1,0:T(8,128)(2,1)} %k_hbm.1, bf16[128,1792]{1,0:T(8,128)(2,1)} %v_hbm.1, bf16[128,1792]{1,0:T(8,128)(2,1)} %c_hbm.1, s32[1,128]{1,0:T(1,128)} %bitcast.1), custom_call_target="tpu_custom_call" | custom-call | flops 308281344 | bytes 3211264 | tf_op jit(solution)/shard_map/pallas_call | solution.py:316
  56.5 2.2 %shard_map.77 = (bf16[128,1792]{1,0:T(8,128)(2,1)}, bf16[128,1792]{1,0:T(8,128)(2,1)}, bf16[128,1792]{1,0:T(8,128)(2,1)}) custom-call(bf16[128,1792]{1,0:T(8,128)(2,1)} %get-tuple-element.6.refs_0_, bf16[128,1792]{1,0:T(8,128)(2,1)} %get-tuple-element.7.refs_1_, bf16[128,1792]{1,0:T(8,128)(2,1)} %get-tuple-element.8.refs_2_), custom_call_target="tpu_custom_call" | custom-call | tf_op jit(solution)/shard_map/pallas_call | solution.py:342
